TPU v7x, 32 devices: a whole 2x2x4 slice. The times are simulated.
32 devices in a mesh: groups: 2 (over y), query: 4 (over z), dim: 4 (over x, core).
Axes of the slice: x: 2, y: 2, z: 4, core: 2. Of those that a mesh axis runs over, the one named last changes fastest.
Arguments:
- query_grads: float32 [64, 262144], P('query', 'dim'), may hold values from -6 to 6
- train_grads: bfloat16 [128, 262144], P(('groups', 'query'), 'dim'), parts along dimension 0, may hold values from -0.01171875 to 0.01171875
- example_ids: int32 [128], P(('groups', 'query')), parts along dimension 0, may hold values from 0 to 4095
- query_ids: int32 [64], P(('query', 'dim')), may hold values from 0 to 4095
- query_norms: float32 [4096], replicated, may hold values from 0.3 to 3
- train_norms: float32 [8192], P('groups'), parts along dimension 0, may hold values from 0.3 to 3
Outputs:
- scores: float32 [128, 64], P(('groups', 'query', 'dim')), parts along dimension 0
There are 2 independent parts, one for each index of `groups`. A program takes and returns all parts, laid end to end along the dimension named above; an argument that names none is the same for every part. Nothing has to cross between parts.
All inputs are finite; a program needn't handle non-finite values.
Results may differ from a plain program's by a relative error of at most 0.0003.
Values may be sent and summed in bfloat16 or wider, within the bound.
A program may use at most 64 MiB of HBM per device.

v0:
```python
import jax
import jax.numpy as jnp
from jax import lax
from jax.sharding import PartitionSpec as P

STEPS = 4


def passed_along(value, axis, by):
    size = lax.axis_size(axis)
    return lax.ppermute(value, axis, [(i, (i + by) % size) for i in range(size)])


def partial_scores(queries, span):
    return lax.dot_general(
        queries,
        span.astype(jnp.float32),
        (((1,), (1,)), ((), ())),
        precision=lax.Precision.HIGHEST,
        preferred_element_type=jnp.float32,
    )


def lookup(table, indices):
    matches = indices[:, None] == lax.iota(jnp.int32, table.shape[0])[None, :]
    return jnp.sum(jnp.where(matches, table[None, :], 0.0), axis=1)


def on_device(query_grads, train_grads, example_ids, query_ids, query_norms, train_norms):
    visited = [(train_grads, example_ids)]
    current = train_grads
    current_ids = example_ids
    for offset in range(1, STEPS):
        current, current_ids = passed_along((current, current_ids), "query", 1)
        visited.append((current, current_ids))
    partials = [partial_scores(query_grads, span) for span, span_ids in visited]
    summed = jnp.concatenate(
        [lax.psum_scatter(piece, "dim", scatter_dimension=0, tiled=True) for piece in partials],
        axis=1,
    )
    seen_ids = jnp.concatenate([span_ids for span, span_ids in visited], axis=0)
    train_scale = lookup(train_norms, seen_ids)
    query_scale = lookup(query_norms, query_ids)
    return summed / (query_scale[:, None] * train_scale[None, :])


def solution(mesh):
    in_specs = (
        P("query", "dim"),
        P(("groups", "query"), "dim"),
        P(("groups", "query")),
        P(("query", "dim")),
        P(),
        P("groups"),
    )
    out_specs = P(("groups", "query", "dim"), None)
    return jax.shard_map(
        on_device, mesh=mesh, in_specs=in_specs, out_specs=out_specs, check_vma=False
    )
```

profile of v0, /device:TPU:0, one launch (start us, length us, event | category | flops | bytes accessed | tf_op | source)
XLA Modules:
  0.0 184.4 jit_solution(9184875663066969479)
XLA Ops:
  0.0 3.0 %collective-permute-start = (bf16[16,65536]{1,0:T(8,128)(2,1)}, bf16[16,65536]{1,0:T(8,128)(2,1)S(1)}, u32[]{:S(2)}, u32[]{:S(2)}) collective-permute-start(bf16[16,65536]{1,0:T(8,128)(2,1)} %param.7), channel_id=1, source_target_pairs={{0,4},{4,8},{8,12},{12,0},{1,5},{5,9},{9,13},{13,1},{2,6},{6,10},{... | collective-permute-start | bytes 6291464 | tf_op jit(solution)/shard_map/ppermute | solution.py:11
  3.0 47.9 %collective-permute-done = bf16[16,65536]{1,0:T(8,128)(2,1)S(1)} collective-permute-done((bf16[16,65536]{1,0:T(8,128)(2,1)}, bf16[16,65536]{1,0:T(8,128)(2,1)S(1)}, u32[]{:S(2)}, u32[]{:S(2)}) %collective-permute-start) | collective-permute-done | bytes 2097184 | tf_op jit(solution)/shard_map/ppermute | solution.py:11
  50.9 0.0 collective-permute-start.1
  50.9 48.7 %collective-permute-done.1 = bf16[16,65536]{1,0:T(8,128)(2,1)} collective-permute-done((bf16[16,65536]{1,0:T(8,128)(2,1)S(1)}, bf16[16,65536]{1,0:T(8,128)(2,1)}, u32[]{:S(2)}, u32[]{:S(2)}) %collective-permute-start.1) | collective-permute-done | bytes 2097184 | tf_op jit(solution)/shard_map/ppermute | solution.py:11
  99.6 0.0 collective-permute-start.2
  99.6 0.0 collective-permute-start.3
  99.6 0.9 select_reduce_fusion.1
  100.5 0.0 copy-start.3
  100.6 0.0 copy-start.2
  100.6 0.0 copy-start.1
  100.6 6.2 %fusion = f32[16,16]{1,0:T(8,128)S(1)} fusion(f32[16,65536]{1,0:T(8,128)} %param.6, bf16[16,65536]{1,0:T(8,128)(2,1)} %param.7), kind=kOutput, calls=%fused_computation.10 | convolution fusion | flops 201326592 | bytes 6292480 | tf_op jit(solution)/shard_map/dot_general | solution.py:15
  106.8 40.8 %collective-permute-done.3 = s32[16]{0:T(128)S(1)} collective-permute-done((s32[16]{0:T(128)}, s32[16]{0:T(128)S(1)}, u32[]{:S(2)}, u32[]{:S(2)}) %collective-permute-start.3) | collective-permute-done | bytes 96 | tf_op jit(solution)/shard_map/ppermute | solution.py:11
  147.6 0.0 collective-permute-start.4
  147.6 0.0 copy-done.3
  147.6 0.6 dynamic-slice
  148.2 4.7 %collective-permute-done.4 = s32[16]{0:T(128)S(1)} collective-permute-done((s32[16]{0:T(128)S(1)}, s32[16]{0:T(128)S(1)}, u32[]{:S(2)}, u32[]{:S(2)}) %collective-permute-start.4) | collective-permute-done | bytes 96 | tf_op jit(solution)/shard_map/ppermute | solution.py:11
  153.0 0.0 collective-permute-start.5
  153.6 4.7 %collective-permute-done.5 = s32[16]{0:T(128)S(1)} collective-permute-done((s32[16]{0:T(128)S(1)}, s32[16]{0:T(128)S(1)}, u32[]{:S(2)}, u32[]{:S(2)}) %collective-permute-start.5) | collective-permute-done | bytes 96 | tf_op jit(solution)/shard_map/ppermute | solution.py:11
  158.3 0.0 copy-done.2
  158.3 0.1 pad_add_fusion
  158.4 0.0 copy-done.1
  158.4 0.3 select_reduce_fusion
  158.7 0.0 copy-start
  158.7 5.0 %fusion.1 = f32[16,16]{1,0:T(8,128)S(1)} fusion(f32[16,65536]{1,0:T(8,128)} %param.6, bf16[16,65536]{1,0:T(8,128)(2,1)S(1)} %collective-permute-done), kind=kOutput, calls=%fused_computation.11 | convolution fusion | flops 201326592 | bytes 6292480 | tf_op jit(solution)/shard_map/dot_general | solution.py:15
  163.7 0.0 copy-done
  163.7 4.8 %fusion.2 = f32[16,16]{1,0:T(8,128)S(1)} fusion(f32[16,65536]{1,0:T(8,128)S(1)} %copy-done, bf16[16,65536]{1,0:T(8,128)(2,1)} %collective-permute-done.1), kind=kOutput, calls=%fused_computation.12 | convolution fusion | flops 201326592 | bytes 6292480 | tf_op jit(solution)/shard_map/dot_general | solution.py:15
  168.5 0.0 collective-permute-done.2
  168.5 4.9 %fusion.3 = f32[16,16]{1,0:T(8,128)S(1)} fusion(f32[16,65536]{1,0:T(8,128)S(1)} %copy-done, bf16[16,65536]{1,0:T(8,128)(2,1)} %collective-permute-done.2), kind=kOutput, calls=%fused_computation.13 | convolution fusion | flops 201326592 | bytes 6292480 | tf_op jit(solution)/shard_map/dot_general | solution.py:15
  173.4 10.3 %all-reduce.4 = (f32[16,16]{1,0:T(8,128)S(1)}, f32[16,16]{1,0:T(8,128)S(1)}, f32[16,16]{1,0:T(8,128)S(1)}, f32[16,16]{1,0:T(8,128)S(1)}) all-reduce(f32[16,16]{1,0:T(8,128)S(1)} %fusion.3, f32[16,16]{1,0:T(8,128)S(1)} %fusion.2, f32[16,16]{1,0:T(8,128)S(1)} %fusion.1, ...), channel_id=5, replica_groups=mesh['groups'=2,'query'=4,'dim'=4] {'dim'}, use_global_device_ids=true, to_apply=%region_3.0.clone | all-reduce | flops 1024 | bytes 8192
  183.8 0.7 maximum_divide_fusion
  (2 shorter events, 0.0 us)
Async XLA Ops:
  0.0 50.9 %collective-permute-start = (bf16[16,65536]{1,0:T(8,128)(2,1)}, bf16[16,65536]{1,0:T(8,128)(2,1)S(1)}, u32[]{:S(2)}, u32[]{:S(2)}) collective-permute-start(bf16[16,65536]{1,0:T(8,128)(2,1)} %param.7), channel_id=1, source_target_pairs={{0,4},{4,8},{8,12},{12,0},{1,5},{5,9},{9,13},{13,1},{2,6},{6,10},{... | collective-permute-start | bytes 6291464 | tf_op jit(solution)/shard_map/ppermute | solution.py:11
  50.9 48.7 %collective-permute-start.1 = (bf16[16,65536]{1,0:T(8,128)(2,1)S(1)}, bf16[16,65536]{1,0:T(8,128)(2,1)}, u32[]{:S(2)}, u32[]{:S(2)}) collective-permute-start(bf16[16,65536]{1,0:T(8,128)(2,1)S(1)} %collective-permute-done), channel_id=1, source_target_pairs={{0,4},{4,8},{8,12},{12,0},{1,5},{5,9},{9,13},{13,1},{2,6},{6,10},{... | collective-permute-start | bytes 6291464 | tf_op jit(solution)/shard_map/ppermute | solution.py:11
  99.6 68.9 %collective-permute-start.2 = (bf16[16,65536]{1,0:T(8,128)(2,1)}, bf16[16,65536]{1,0:T(8,128)(2,1)}, u32[]{:S(2)}, u32[]{:S(2)}) collective-permute-start(bf16[16,65536]{1,0:T(8,128)(2,1)} %collective-permute-done.1), channel_id=1, source_target_pairs={{0,4},{4,8},{8,12},{12,0},{1,5},{5,9},{9,13},{13,1},{2,6},{6,10},{... | collective-permute-start | bytes 6291464 | tf_op jit(solution)/shard_map/ppermute | solution.py:11
  99.6 48.0 %collective-permute-start.3 = (s32[16]{0:T(128)}, s32[16]{0:T(128)S(1)}, u32[]{:S(2)}, u32[]{:S(2)}) collective-permute-start(s32[16]{0:T(128)} %param.8), channel_id=1, source_target_pairs={{0,4},{4,8},{8,12},{12,0},{1,5},{5,9},{9,13},{13,1},{2,6},{6,10},{... | collective-permute-start | bytes 200 | tf_op jit(solution)/shard_map/ppermute | solution.py:11
  100.5 47.1 %copy-start.3 = (u32[32]{0:T(128)S(1)}, u32[32]{0:T(128)}, u32[]{:S(2)}) copy-start(u32[32]{0:T(128)} %constant.5) | copy-start | bytes 388
  100.6 57.7 %copy-start.2 = (s32[16]{0:T(128)S(1)}, s32[16]{0:T(128)}, u32[]{:S(2)}) copy-start(s32[16]{0:T(128)} %param.8) | copy-start | bytes 196
  100.6 57.8 %copy-start.1 = (f32[4096]{0:T(1024)S(1)}, f32[4096]{0:T(1024)}, u32[]{:S(2)}) copy-start(f32[4096]{0:T(1024)} %param.11) | copy-start | bytes 49156
  147.6 5.3 %collective-permute-start.4 = (s32[16]{0:T(128)S(1)}, s32[16]{0:T(128)S(1)}, u32[]{:S(2)}, u32[]{:S(2)}) collective-permute-start(s32[16]{0:T(128)S(1)} %collective-permute-done.3), channel_id=1, source_target_pairs={{0,4},{4,8},{8,12},{12,0},{1,5},{5,9},{9,13},{13,1},{2,6},{6,10},{... | collective-permute-start | bytes 200 | tf_op jit(solution)/shard_map/ppermute | solution.py:11
  153.0 5.3 %collective-permute-start.5 = (s32[16]{0:T(128)S(1)}, s32[16]{0:T(128)S(1)}, u32[]{:S(2)}, u32[]{:S(2)}) collective-permute-start(s32[16]{0:T(128)S(1)} %collective-permute-done.4), channel_id=1, source_target_pairs={{0,4},{4,8},{8,12},{12,0},{1,5},{5,9},{9,13},{13,1},{2,6},{6,10},{... | collective-permute-start | bytes 200 | tf_op jit(solution)/shard_map/ppermute | solution.py:11
  158.7 5.0 %copy-start = (f32[16,65536]{1,0:T(8,128)S(1)}, f32[16,65536]{1,0:T(8,128)}, u32[]{:S(2)}) copy-start(f32[16,65536]{1,0:T(8,128)} %param.6) | copy-start | bytes 12582916
where the time goes:
time: 185 us; the launch traced here: 184 us
  waiting for transfers between devices  147 us (79%)
  matrix products  20.9 us (11%)
  blocking collectives  10.3 us (6%)
  starting transfers between devices  3.04 us (2%)
  other arithmetic  1.97 us (1%)
    ppermute x6, waiting for transfers between devices, passed_along(): lax.ppermute(value, axis, [(i, (i + by) % size) for i in range(size)])  147 us
    dot_general x4, matrix products, partial_scores(): lax.dot_general(queries, span.astype(jnp.float32), (((1,), (1,)), ((), ()...  20.9 us
    unnamed x1, blocking collectives  10.3 us
  transfers between devices with their start and end apart: 6, of which 5 were waited for; matrix products, arithmetic and copies ran while one was open for 10% of the time, Pallas kernels for 0%

commit v1 on v0

--- a/solution.py
+++ b/solution.py
@@ -1,9 +1,16 @@
+import functools
+
 import jax
 import jax.numpy as jnp
 from jax import lax
+from jax.experimental import pallas as pl
+from jax.experimental.pallas import tpu as pltpu
 from jax.sharding import PartitionSpec as P
 
 STEPS = 4
+WIDTH = 2048
+FULL = 32767.0
+MESH = pl.DeviceIdType.MESH
 
 
 def passed_along(value, axis, by):
@@ -44,6 +51,359 @@
     return summed / (query_scale[:, None] * train_scale[None, :])
 
 
+def kernel(
+    sizes, width, wide,
+    q_ref, t_ref, eid_ref, qid_ref, qn_ref, tn_ref, out_ref,
+    qf, code, tb, acc, scales, part, part_in, final, final_in,
+    local_sem, own_send, fwd_send, q_recv, t_send, t_recv,
+    scale_send, scale_recv, part_send, part_recv, final_send, final_recv,
+):
+    groups, steps, dims = sizes
+    rows = q_ref.shape[0]
+    mine = rows // dims
+    half = qf.shape[1]
+    chunks = half // width
+    y, z, d = lax.axis_index("groups"), lax.axis_index("query"), lax.axis_index("dim")
+    other_y = 1 - y
+    high = z // 2
+    is_inner = jnp.logical_or(z == 1, z == 2)
+    partner = jnp.where(high == 0, 1 - z, 5 - z)
+    end = jnp.where(high == 0, 0, 3)
+    far_inner = jnp.where(high == 0, 2, 1)
+    far_end = jnp.where(high == 0, 3, 0)
+    plane = groups * dims
+    place = y * dims + d
+
+    def cols(c, base=0):
+        return pl.ds(pl.multiple_of(base + c * width, width), width)
+
+    def remote(src, dst, send, recv, to):
+        return pltpu.make_async_remote_copy(
+            src_ref=src, dst_ref=dst, send_sem=send, recv_sem=recv,
+            device_id=to, device_id_type=MESH,
+        )
+
+    def send_code(block, c, to_z, send):
+        view = code.at[block, :, cols(c)]
+        return remote(view, view, send, q_recv.at[block, c], (y, to_z, d))
+
+    def got_code(block, c):
+        send_code(block, c, partner, own_send.at[0, c]).wait_recv()
+
+    def send_train(c, half_of, slot, send, to):
+        return remote(
+            t_ref.at[:, cols(c, half_of * half)],
+            tb.at[pl.ds(pl.multiple_of(slot * rows, rows), rows), cols(c)],
+            send, t_recv.at[slot, c], to,
+        )
+
+    def got_train(slot, c):
+        send_train(c, y, slot, t_send.at[0, c], (y, partner, d)).wait_recv()
+
+    across = [(c, other_y, y, t_send.at[0, c], (other_y, z, d)) for c in range(chunks)]
+    diagonal = [(c, other_y, 2 + y, t_send.at[0, c], (other_y, partner, d)) for c in range(chunks)]
+    straight = [(c, y, 2 + y, t_send.at[1, c], (y, partner, d)) for c in range(chunks)]
+
+    load_q = pltpu.make_async_copy(
+        q_ref.at[:, pl.ds(pl.multiple_of(y * half, half), half)], qf, local_sem.at[0])
+    load_t = pltpu.make_async_copy(
+        t_ref.at[:, pl.ds(pl.multiple_of(y * half, half), half)],
+        tb.at[pl.ds(pl.multiple_of(y * rows, rows), rows), :], local_sem.at[1])
+    load_q.start()
+    load_t.start()
+
+    barrier = pltpu.get_barrier_semaphore()
+    peers = []
+    for step in range(1, plane):
+        at = lax.rem(place + step, plane)
+        peers.append((at // dims, z, lax.rem(at, dims)))
+    for step in range(1, steps):
+        peers.append((y, lax.rem(z + step, steps), d))
+    peers.append((other_y, partner, d))
+    for peer in peers:
+        pl.semaphore_signal(barrier, inc=1, device_id=peer, device_id_type=MESH)
+    pl.semaphore_wait(barrier, len(peers))
+
+    @pl.when(is_inner)
+    def _():
+        for args in across:
+            send_train(*args).start()
+
+    @pl.when(jnp.logical_not(is_inner))
+    def _():
+        for args in across[:wide]:
+            send_train(*args).start()
+
+    load_q.wait()
+
+    def largest(c, most):
+        return jnp.maximum(most, jnp.max(jnp.abs(qf[:, cols(c)]), axis=1, keepdims=True))
+
+    top = jnp.maximum(lax.fori_loop(0, chunks, largest, jnp.zeros((rows, 1), jnp.float32)), 1e-30)
+    scales[z] = jnp.broadcast_to(top * (1.0 / (FULL * FULL)), (rows, 128))
+    inverse = 1.0 / top
+
+    def encode(c):
+        x = qf[:, cols(c)]
+        size = (jnp.sqrt(jnp.abs(x) * inverse) * FULL + 0.5).astype(jnp.int32)
+        code[z, :, cols(c)] = jnp.where(x < 0, -size, size).astype(jnp.int16)
+
+    def encode_wide(c, carry):
+        encode(c)
+        send_code(z, c, partner, own_send.at[0, c]).start()
+
+        @pl.when(is_inner)
+        def _():
+            send_code(z, c, far_inner, own_send.at[1, c]).start()
+        return carry
+
+    lax.fori_loop(0, wide, encode_wide, 0)
+
+    def send_scale(step):
+        return remote(
+            scales.at[z], scales.at[z], scale_send.at[step - 1], scale_recv.at[z],
+            (y, lax.rem(z + step, steps), d))
+
+    for step in range(1, steps):
+        send_scale(step).start()
+
+    def encode_rest(c, carry):
+        encode(c)
+
+        @pl.when(jnp.logical_not(is_inner))
+        def _():
+            send_code(z, c, partner, own_send.at[0, c]).start()
+        return carry
+
+    lax.fori_loop(wide, chunks, encode_rest, 0)
+
+    def pick(table, ids):
+        at = lax.broadcasted_iota(jnp.int32, (ids.shape[0], table.shape[1]), 1)
+        return jnp.sum(jnp.where(at == ids, table, 0.0), axis=1, keepdims=True)
+
+    def column(ids):
+        count = ids.shape[1]
+        square = (count, count)
+        same = lax.broadcasted_iota(jnp.int32, square, 0) == lax.broadcasted_iota(jnp.int32, square, 1)
+        wide_ids = jnp.broadcast_to(ids.astype(jnp.float32), square)
+        return jnp.sum(jnp.where(same, wide_ids, 0.0), axis=1, keepdims=True).astype(jnp.int32)
+
+    span = steps * rows
+    train_scale = pick(tn_ref[...], column(eid_ref[...]))
+    lane = lax.broadcasted_iota(jnp.int32, (rows, span), 1)
+    own_lane = lax.rem(lane, rows) == lax.broadcasted_iota(jnp.int32, (rows, span), 0)
+    train_row = jnp.sum(jnp.where(own_lane, train_scale, 0.0), axis=0, keepdims=True)
+    query_scale = pick(qn_ref[...], column(qid_ref[...]))
+
+    acc[...] = jnp.zeros_like(acc)
+    load_t.wait()
+
+    def multiply(c, held):
+        coded = code[:, :, cols(c)].reshape(steps * rows, width).astype(jnp.int32).astype(jnp.float32)
+        value = coded * jnp.abs(coded)
+        upper = value.astype(jnp.bfloat16)
+        lower = (value - upper.astype(jnp.float32)).astype(jnp.bfloat16)
+        acc[:, :held] += lax.dot_general(
+            jnp.concatenate([upper, lower], axis=0), tb[:held, cols(c)],
+            (((1,), (1,)), ((), ())), preferred_element_type=jnp.float32,
+        )
+
+    narrow = groups * rows
+
+    @pl.when(jnp.logical_not(is_inner))
+    def _():
+        for args in straight[wide:] + diagonal[wide:]:
+            send_train(*args).start()
+
+        def visit(c, carry):
+            got_code(partner, c)
+            got_code(far_inner, c)
+            got_code(far_end, c)
+            got_train(other_y, c)
+            multiply(c, narrow)
+            return carry
+
+        lax.fori_loop(0, wide, visit, 0)
+
+        def sent(c, carry):
+            send_code(z, c, partner, own_send.at[0, c]).wait_send()
+            return carry
+
+        lax.fori_loop(0, chunks, sent, 0)
+        for args in across[:wide] + straight[wide:] + diagonal[wide:]:
+            send_train(*args).wait_send()
+
+    @pl.when(is_inner)
+    def _():
+        def pass_on(c, carry):
+            got_code(end, c)
+            send_code(end, c, far_inner, fwd_send.at[0, c]).start()
+            got_code(far_inner, c)
+            send_code(far_inner, c, end, fwd_send.at[1, c]).start()
+            return carry
+
+        lax.fori_loop(0, wide, pass_on, 0)
+
+        def rest(c, carry):
+            send_code(z, c, far_inner, own_send.at[1, c]).start()
+            return carry
+
+        lax.fori_loop(wide, chunks, rest, 0)
+
+        def visit(c, carry):
+            got_code(far_end, c)
+            send_code(far_end, c, end, fwd_send.at[2, c]).start()
+
+            @pl.when(c < chunks - wide)
+            def _():
+                got_code(end, wide + c)
+                send_code(end, wide + c, far_inner, fwd_send.at[0, wide + c]).start()
+
+            got_train(other_y, c)
+            multiply(c, narrow)
+            return carry
+
+        lax.fori_loop(0, wide, visit, 0)
+
+        def close(c, carry):
+            got_code(far_inner, c)
+            got_code(far_end, c)
+            got_train(other_y, c)
+            got_train(2 + y, c)
+            got_train(2 + other_y, c)
+            multiply(c, 2 * narrow)
+            return carry
+
+        lax.fori_loop(wide, chunks, close, 0)
+
+        def sent(c, carry):
+            send_code(z, c, far_inner, own_send.at[1, c]).wait_send()
+            send_code(end, c, far_inner, fwd_send.at[0, c]).wait_send()
+            return carry
+
+        lax.fori_loop(0, chunks, sent, 0)
+
+        def sent_wide(c, carry):
+            send_code(z, c, end, own_send.at[0, c]).wait_send()
+            send_code(far_inner, c, end, fwd_send.at[1, c]).wait_send()
+            send_code(far_end, c, end, fwd_send.at[2, c]).wait_send()
+            return carry
+
+        lax.fori_loop(0, wide, sent_wide, 0)
+        for args in across:
+            send_train(*args).wait_send()
+
+    for step in range(1, steps):
+        send_scale(step).wait_send()
+        source = lax.rem(z + step, steps)
+        remote(scales.at[source], scales.at[source], scale_send.at[0], scale_recv.at[source],
+               (y, source, d)).wait_recv()
+
+    lane_block = lane // rows
+    for b in range(steps):
+        at = pl.ds(b * rows, rows)
+        product = (acc[at, :] + acc[pl.ds((steps + b) * rows, rows), :]) * scales[b][:, :1]
+        near_at = lane_block == lax.rem(b - z + steps, steps)
+        end_at = lane_block == lax.rem(b - end + steps, steps)
+        for g in range(groups):
+            near = jnp.concatenate([product[:, g * rows:(g + 1) * rows]] * steps, axis=1)
+            far = jnp.concatenate([product[:, narrow + g * rows:narrow + (g + 1) * rows]] * steps, axis=1)
+            block = jnp.where(near_at, near, 0.0) + jnp.where(end_at, far, 0.0)
+            for to in range(dims):
+                part[g * dims + to, pl.ds(b * mine, mine), :span] = block[to * mine:(to + 1) * mine]
+
+    def send_part(step):
+        at = lax.rem(place + step, plane)
+        return remote(part.at[at], part_in.at[place], part_send.at[step - 1], part_recv.at[place],
+                      (at // dims, z, lax.rem(at, dims)))
+
+    def got_part(step):
+        at = lax.rem(place + step, plane)
+        remote(part.at[at], part_in.at[at], part_send.at[step - 1], part_recv.at[at],
+               (at // dims, z, lax.rem(at, dims))).wait_recv()
+
+    for step in range(1, plane):
+        send_part(step).start()
+    total = part[place]
+    for step in range(1, plane):
+        got_part(step)
+        total = total + part_in[lax.rem(place + step, plane)]
+
+    for b in range(steps):
+        final[b, :mine, :] = total[b * mine:(b + 1) * mine]
+        first = lane_block[:1] == lax.rem(b - z + steps, steps)
+        final[b, mine:mine + 1, :span] = jnp.where(first, train_row, 0.0)
+
+    def send_final(step):
+        at = lax.rem(z + step, steps)
+        return remote(final.at[at], final_in.at[z], final_send.at[step - 1], final_recv.at[z], (y, at, d))
+
+    def got_final(step):
+        at = lax.rem(z + step, steps)
+        remote(final.at[at], final_in.at[at], final_send.at[step - 1], final_recv.at[at],
+               (y, at, d)).wait_recv()
+
+    for step in range(1, steps):
+        send_final(step).start()
+    summed = final[z]
+    for step in range(1, steps):
+        got_final(step)
+        summed = summed + final_in[lax.rem(z + step, steps)]
+    out_ref[...] = summed[:mine, :span] / (query_scale * summed[mine:mine + 1, :span])
+
+    for step in range(1, plane):
+        send_part(step).wait_send()
+    for step in range(1, steps):
+        send_final(step).wait_send()
+
+
+def all_pairs(sizes, query_grads, train_grads, example_ids, query_ids, query_norms, train_norms):
+    groups, steps, dims = sizes
+    rows, depth = query_grads.shape
+    half = depth // groups
+    width = min(WIDTH, half // 8)
+    chunks = half // width
+    wide = (chunks * 5) // 8
+    plane = groups * dims
+    dma, vmem = pltpu.SemaphoreType.DMA, pltpu.VMEM
+    whole = pl.BlockSpec(memory_space=pltpu.VMEM)
+    anywhere = pl.BlockSpec(memory_space=pl.ANY)
+    return pl.pallas_call(
+        functools.partial(kernel, sizes, width, wide),
+        out_shape=jax.ShapeDtypeStruct((rows // dims, steps * rows), jnp.float32),
+        in_specs=[anywhere, anywhere, whole, whole, whole, whole],
+        out_specs=whole,
+        scratch_shapes=[
+            vmem((rows, half), jnp.float32),
+            vmem((steps, rows, half), jnp.int16),
+            vmem((2 * groups * rows, half), jnp.bfloat16),
+            vmem((2 * steps * rows, 2 * groups * rows), jnp.float32),
+            vmem((steps, rows, 128), jnp.float32),
+            vmem((plane, rows, 128), jnp.float32),
+            vmem((plane, rows, 128), jnp.float32),
+            vmem((steps, 8, 128), jnp.float32),
+            vmem((steps, 8, 128), jnp.float32),
+            dma((2,)),
+            dma((2, chunks)),
+            dma((3, chunks)),
+            dma((steps, chunks)),
+            dma((2, chunks)),
+            dma((2 * groups, chunks)),
+            dma((steps - 1,)),
+            dma((steps,)),
+            dma((plane - 1,)),
+            dma((plane,)),
+            dma((steps - 1,)),
+            dma((steps,)),
+        ],
+        compiler_params=pltpu.CompilerParams(
+            collective_id=0, has_side_effects=True, vmem_limit_bytes=32 * 1024 * 1024),
+    )(
+        query_grads, train_grads, example_ids.reshape(1, -1), query_ids.reshape(1, -1),
+        query_norms.reshape(1, -1), train_norms.reshape(1, -1),
+    )
+
+
 def solution(mesh):
     in_specs = (
         P("query", "dim"),
@@ -54,6 +414,8 @@
         P("groups"),
     )
     out_specs = P(("groups", "query", "dim"), None)
+    sizes = tuple(mesh.shape[axis] for axis in ("groups", "query", "dim"))
+    body = functools.partial(all_pairs, sizes) if sizes[:2] == (2, STEPS) else on_device
     return jax.shard_map(
-        on_device, mesh=mesh, in_specs=in_specs, out_specs=out_specs, check_vma=False
+        body, mesh=mesh, in_specs=in_specs, out_specs=out_specs, check_vma=False
     )

time: 185 us -> 71.2 us (0.38)
  waiting for transfers between devices: 147 us -> 0 us
  Pallas kernels: 0 us -> 63.8 us
  matrix products: 20.9 us -> 0 us
  blocking collectives: 10.3 us -> 0 us
  local copies, waits for them, and re-layouts: 0.63 us -> 7.1 us
  starting transfers between devices: 3.04 us -> 0 us
  other arithmetic: 1.97 us -> 0 us
    ppermute x6 -> x0, waiting for transfers between devices: 147 us -> none  [passed_along(): lax.ppermute(value, axis, [(i, (i + by) % size) for i in range(size)])]
    pallas_call x0 -> x1, Pallas kernels: none -> 63.8 us  [all_pairs(): pl.pallas_call(functools.partial(kernel, sizes, width, wide), out_shape=j...]
    dot_general x4 -> x0, matrix products: 20.9 us -> none  [partial_scores(): lax.dot_general(queries, span.astype(jnp.float32), (((1,), (1,)), ((), ()...]
    unnamed x1 -> x0, blocking collectives: 10.3 us -> none
    unnamed x11 -> x13, local copies, waits for them, and re-layouts: 0.63 us -> 7.1 us
    ppermute x6 -> x0, starting transfers between devices: 3.04 us -> none  [passed_along(): lax.ppermute(value, axis, [(i, (i + by) % size) for i in range(size)])]
  transfers between devices with their start and end apart: 6 -> 0, of which waited for: 5 -> 0; matrix products, arithmetic and copies ran while one was open for 10% -> 0% of each run, Pallas kernels for 0% -> 0%
where the time goes in v1:
time: 71.2 us; the launch traced here: 70.9 us
  Pallas kernels  63.8 us (90%)
  local copies, waits for them, and re-layouts  7.1 us (10%)
    pallas_call x1, Pallas kernels, all_pairs(): pl.pallas_call(functools.partial(kernel, sizes, width, wide), out_shape=j...  63.8 us
    unnamed x13, local copies, waits for them, and re-layouts  7.1 us

profile of v1, /device:TPU:0, one launch (start us, length us, event | category | flops | bytes accessed | tf_op | source)
XLA Modules:
  0.0 70.9 jit_solution(18207725736073485121)
XLA Ops:
  0.0 0.0 copy-start
  0.0 2.2 %copy-done = f32[16,65536]{1,0:T(8,128)S(1)} copy-done((f32[16,65536]{1,0:T(8,128)S(1)}, f32[16,65536]{1,0:T(8,128)}, u32[]{:S(2)}) %copy-start) | copy-done | bytes 4194328
  2.2 0.0 copy-start.1
  2.2 1.6 %copy-done.1 = bf16[16,65536]{1,0:T(8,128)(2,1)S(1)} copy-done((bf16[16,65536]{1,0:T(8,128)(2,1)S(1)}, bf16[16,65536]{1,0:T(8,128)(2,1)}, u32[]{:S(2)}) %copy-start.1) | copy-done | bytes 2097176
  3.8 0.0 copy-start.2
  3.8 0.7 %copy-done.2 = f32[4096]{0:T(1024)S(1)} copy-done((f32[4096]{0:T(1024)S(1)}, f32[4096]{0:T(1024)}, u32[]{:S(2)}) %copy-start.2) | copy-done | bytes 16408
  4.5 0.0 copy-start.3
  4.5 0.7 %copy-done.3 = f32[4096]{0:T(1024)S(1)} copy-done((f32[4096]{0:T(1024)S(1)}, f32[4096]{0:T(1024)}, u32[]{:S(2)}) %copy-start.3) | copy-done | bytes 16408
  5.2 0.0 copy-start.4
  5.2 0.7 copy-done.4
  5.9 0.0 copy-start.5
  5.9 0.7 copy-done.5
  6.5 63.8 %shard_map.64 = f32[4,64]{1,0:T(4,128)S(1)} custom-call(f32[16,65536]{1,0:T(8,128)S(1)} %copy-done, bf16[16,65536]{1,0:T(8,128)(2,1)S(1)} %copy-done.1, s32[1,16]{1,0:T(1,128)S(1)} %bitcast.6, s32[1,4]{1,0:T(1,128)S(1)} %bitcast.7, f32[1,4096]{1,0:T(1,128)S(1)} %bitcast.4, f32[1,4096]{1,0:T(1,128)S(1)} %bitcast.5), custom_call_target="tpu_custom_call" | custom-call | tf_op jit(solution)/shard_map/pallas_call | solution.py:371
  70.3 0.6 copy.8
Async XLA Ops:
  0.0 2.2 %copy-start = (f32[16,65536]{1,0:T(8,128)S(1)}, f32[16,65536]{1,0:T(8,128)}, u32[]{:S(2)}) copy-start(f32[16,65536]{1,0:T(8,128)} %q_ref.1) | copy-start | bytes 12582916
  2.2 1.6 %copy-start.1 = (bf16[16,65536]{1,0:T(8,128)(2,1)S(1)}, bf16[16,65536]{1,0:T(8,128)(2,1)}, u32[]{:S(2)}) copy-start(bf16[16,65536]{1,0:T(8,128)(2,1)} %t_ref.1) | copy-start | bytes 6291460
  3.8 0.7 %copy-start.2 = (f32[4096]{0:T(1024)S(1)}, f32[4096]{0:T(1024)}, u32[]{:S(2)}) copy-start(f32[4096]{0:T(1024)} %param.10) | copy-start | bytes 49156
  4.5 0.7 %copy-start.3 = (f32[4096]{0:T(1024)S(1)}, f32[4096]{0:T(1024)}, u32[]{:S(2)}) copy-start(f32[4096]{0:T(1024)} %param.11) | copy-start | bytes 49156
  5.2 0.7 copy-start.4
  5.9 0.7 copy-start.5

commit v2 on v1

--- a/solution.py
+++ b/solution.py
@@ -8,7 +8,7 @@
 from jax.sharding import PartitionSpec as P
 
 STEPS = 4
-WIDTH = 2048
+WIDTH = 4096
 FULL = 32767.0
 MESH = pl.DeviceIdType.MESH
 
@@ -53,10 +53,10 @@
 
 def kernel(
     sizes, width, wide,
-    q_ref, t_ref, eid_ref, qid_ref, qn_ref, tn_ref, out_ref,
-    qf, code, tb, acc, scales, part, part_in, final, final_in,
+    q_ref, t_ref, eid_hbm, qid_hbm, qn_hbm, tn_hbm, out_ref,
+    qf, eid_ref, qid_ref, qn_ref, tn_ref, code, tb, acc, scales, tiles, tiles_in,
     local_sem, own_send, fwd_send, q_recv, t_send, t_recv,
-    scale_send, scale_recv, part_send, part_recv, final_send, final_recv,
+    scale_send, scale_recv, tile_send, tile_recv,
 ):
     groups, steps, dims = sizes
     rows = q_ref.shape[0]
@@ -72,7 +72,7 @@
     far_inner = jnp.where(high == 0, 2, 1)
     far_end = jnp.where(high == 0, 3, 0)
     plane = groups * dims
-    place = y * dims + d
+    in_plane = y * dims + d
 
     def cols(c, base=0):
         return pl.ds(pl.multiple_of(base + c * width, width), width)
@@ -111,11 +111,18 @@
         tb.at[pl.ds(pl.multiple_of(y * rows, rows), rows), :], local_sem.at[1])
     load_q.start()
     load_t.start()
+    tables = [
+        pltpu.make_async_copy(src, dst, local_sem.at[2 + at])
+        for at, (src, dst) in enumerate(
+            [(eid_hbm, eid_ref), (qid_hbm, qid_ref), (qn_hbm, qn_ref), (tn_hbm, tn_ref)])
+    ]
+    for table in tables:
+        table.start()
 
     barrier = pltpu.get_barrier_semaphore()
     peers = []
     for step in range(1, plane):
-        at = lax.rem(place + step, plane)
+        at = lax.rem(in_plane + step, plane)
         peers.append((at // dims, z, lax.rem(at, dims)))
     for step in range(1, steps):
         peers.append((y, lax.rem(z + step, steps), d))
@@ -188,10 +195,12 @@
         wide_ids = jnp.broadcast_to(ids.astype(jnp.float32), square)
         return jnp.sum(jnp.where(same, wide_ids, 0.0), axis=1, keepdims=True).astype(jnp.int32)
 
+    for table in tables:
+        table.wait()
+    train_scale = pick(tn_ref[...], column(eid_ref[...]))
     span = steps * rows
-    train_scale = pick(tn_ref[...], column(eid_ref[...]))
-    lane = lax.broadcasted_iota(jnp.int32, (rows, span), 1)
-    own_lane = lax.rem(lane, rows) == lax.broadcasted_iota(jnp.int32, (rows, span), 0)
+    lane = lax.broadcasted_iota(jnp.int32, (rows, 128), 1)
+    own_lane = lane == lax.broadcasted_iota(jnp.int32, (rows, 128), 0) + 2 * groups * rows
     train_row = jnp.sum(jnp.where(own_lane, train_scale, 0.0), axis=0, keepdims=True)
     query_scale = pick(qn_ref[...], column(qid_ref[...]))
 
@@ -210,6 +219,47 @@
 
     narrow = groups * rows
 
+    around = [
+        [lax.rem(at + step, size) for step in range(size)]
+        for at, size in zip((y, z, d), sizes)
+    ]
+    peers_all = [
+        (to_y, to_z, to_d)
+        for at_z, to_z in enumerate(around[1])
+        for at_y, to_y in enumerate(around[0])
+        for at_d, to_d in enumerate(around[2])
+        if at_y + at_z + at_d
+    ]
+
+    def slot(peer):
+        return (peer[0] * steps + peer[1]) * dims + peer[2]
+
+    place = slot((y, z, d))
+
+    def send_tile(at):
+        peer = peers_all[at]
+        return remote(tiles.at[peer[1] * dims + peer[2]], tiles_in.at[place],
+                      tile_send.at[at], tile_recv.at[place], peer)
+
+    def got_tile(at):
+        peer = peers_all[at]
+        remote(tiles.at[peer[1] * dims + peer[2]], tiles_in.at[slot(peer)],
+               tile_send.at[at], tile_recv.at[slot(peer)], peer).wait_recv()
+
+    def give_tiles():
+        for step in range(1, steps):
+            source = lax.rem(z + step, steps)
+            remote(scales.at[source], scales.at[source], scale_send.at[0], scale_recv.at[source],
+                   (y, source, d)).wait_recv()
+        for b in range(steps):
+            pieces = acc[pl.ds(b * rows, rows), :] + acc[pl.ds((steps + b) * rows, rows), :]
+            product = pieces * scales[b] + train_row
+            for to in range(dims):
+                tiles[b * dims + to] = product[to * mine:(to + 1) * mine]
+        for at in range(len(peers_all)):
+            send_tile(at).start()
+        tiles_in[place] = tiles[z * dims + d]
+
     @pl.when(jnp.logical_not(is_inner))
     def _():
         for args in straight[wide:] + diagonal[wide:]:
@@ -224,14 +274,7 @@
             return carry
 
         lax.fori_loop(0, wide, visit, 0)
-
-        def sent(c, carry):
-            send_code(z, c, partner, own_send.at[0, c]).wait_send()
-            return carry
-
-        lax.fori_loop(0, chunks, sent, 0)
-        for args in across[:wide] + straight[wide:] + diagonal[wide:]:
-            send_train(*args).wait_send()
+        give_tiles()
 
     @pl.when(is_inner)
     def _():
@@ -275,7 +318,41 @@
             return carry
 
         lax.fori_loop(wide, chunks, close, 0)
-
+        give_tiles()
+
+    for at in range(len(peers_all)):
+        got_tile(at)
+    by_source = tiles_in[...].reshape(groups, steps, dims, mine, 128)
+    summed = jnp.sum(jnp.sum(by_source, axis=2), axis=0)
+
+    def lanes_of(block, role):
+        first = [(role * groups + g) * rows for g in range(groups)]
+        return jnp.where(y == 0, block[:, first[0]:first[0] + rows], block[:, first[1]:first[1] + rows])
+
+    raw = [lanes_of(summed[k], 0) for k in range(steps)]
+    raw[0] = raw[0] + lanes_of(summed[1], 1)
+    raw[3] = raw[3] + lanes_of(summed[2], 1)
+    lane_block = lax.broadcasted_iota(jnp.int32, (mine, span), 1) // rows
+    scores = jnp.zeros((mine, span), jnp.float32)
+    for k in range(steps):
+        train = tiles_in[slot((y, k, d))][:, 2 * groups * rows:2 * groups * rows + rows]
+        value = raw[k] / (query_scale * train)
+        here = lane_block == lax.rem(z - k + steps, steps)
+        scores = scores + jnp.where(here, jnp.concatenate([value] * steps, axis=1), 0.0)
+    out_ref[...] = scores
+
+    @pl.when(jnp.logical_not(is_inner))
+    def _():
+        def sent(c, carry):
+            send_code(z, c, partner, own_send.at[0, c]).wait_send()
+            return carry
+
+        lax.fori_loop(0, chunks, sent, 0)
+        for args in across[:wide] + straight[wide:] + diagonal[wide:]:
+            send_train(*args).wait_send()
+
+    @pl.when(is_inner)
+    def _():
         def sent(c, carry):
             send_code(z, c, far_inner, own_send.at[1, c]).wait_send()
             send_code(end, c, far_inner, fwd_send.at[0, c]).wait_send()
@@ -295,66 +372,8 @@
 
     for step in range(1, steps):
         send_scale(step).wait_send()
-        source = lax.rem(z + step, steps)
-        remote(scales.at[source], scales.at[source], scale_send.at[0], scale_recv.at[source],
-               (y, source, d)).wait_recv()
-
-    lane_block = lane // rows
-    for b in range(steps):
-        at = pl.ds(b * rows, rows)
-        product = (acc[at, :] + acc[pl.ds((steps + b) * rows, rows), :]) * scales[b][:, :1]
-        near_at = lane_block == lax.rem(b - z + steps, steps)
-        end_at = lane_block == lax.rem(b - end + steps, steps)
-        for g in range(groups):
-            near = jnp.concatenate([product[:, g * rows:(g + 1) * rows]] * steps, axis=1)
-            far = jnp.concatenate([product[:, narrow + g * rows:narrow + (g + 1) * rows]] * steps, axis=1)
-            block = jnp.where(near_at, near, 0.0) + jnp.where(end_at, far, 0.0)
-            for to in range(dims):
-                part[g * dims + to, pl.ds(b * mine, mine), :span] = block[to * mine:(to + 1) * mine]
-
-    def send_part(step):
-        at = lax.rem(place + step, plane)
-        return remote(part.at[at], part_in.at[place], part_send.at[step - 1], part_recv.at[place],
-                      (at // dims, z, lax.rem(at, dims)))
-
-    def got_part(step):
-        at = lax.rem(place + step, plane)
-        remote(part.at[at], part_in.at[at], part_send.at[step - 1], part_recv.at[at],
-               (at // dims, z, lax.rem(at, dims))).wait_recv()
-
-    for step in range(1, plane):
-        send_part(step).start()
-    total = part[place]
-    for step in range(1, plane):
-        got_part(step)
-        total = total + part_in[lax.rem(place + step, plane)]
-
-    for b in range(steps):
-        final[b, :mine, :] = total[b * mine:(b + 1) * mine]
-        first = lane_block[:1] == lax.rem(b - z + steps, steps)
-        final[b, mine:mine + 1, :span] = jnp.where(first, train_row, 0.0)
-
-    def send_final(step):
-        at = lax.rem(z + step, steps)
-        return remote(final.at[at], final_in.at[z], final_send.at[step - 1], final_recv.at[z], (y, at, d))
-
-    def got_final(step):
-        at = lax.rem(z + step, steps)
-        remote(final.at[at], final_in.at[at], final_send.at[step - 1], final_recv.at[at],
-               (y, at, d)).wait_recv()
-
-    for step in range(1, steps):
-        send_final(step).start()
-    summed = final[z]
-    for step in range(1, steps):
-        got_final(step)
-        summed = summed + final_in[lax.rem(z + step, steps)]
-    out_ref[...] = summed[:mine, :span] / (query_scale * summed[mine:mine + 1, :span])
-
-    for step in range(1, plane):
-        send_part(step).wait_send()
-    for step in range(1, steps):
-        send_final(step).wait_send()
+    for at in range(len(peers_all)):
+        send_tile(at).wait_send()
 
 
 def all_pairs(sizes, query_grads, train_grads, example_ids, query_ids, query_norms, train_norms):
@@ -367,23 +386,25 @@
     plane = groups * dims
     dma, vmem = pltpu.SemaphoreType.DMA, pltpu.VMEM
     whole = pl.BlockSpec(memory_space=pltpu.VMEM)
-    anywhere = pl.BlockSpec(memory_space=pl.ANY)
+    in_hbm = pl.BlockSpec(memory_space=pltpu.HBM)
     return pl.pallas_call(
         functools.partial(kernel, sizes, width, wide),
         out_shape=jax.ShapeDtypeStruct((rows // dims, steps * rows), jnp.float32),
-        in_specs=[anywhere, anywhere, whole, whole, whole, whole],
+        in_specs=[in_hbm] * 6,
         out_specs=whole,
         scratch_shapes=[
             vmem((rows, half), jnp.float32),
+            vmem((1, example_ids.shape[0]), jnp.int32),
+            vmem((1, query_ids.shape[0]), jnp.int32),
+            vmem((1, query_norms.shape[0]), jnp.float32),
+            vmem((1, train_norms.shape[0]), jnp.float32),
             vmem((steps, rows, half), jnp.int16),
             vmem((2 * groups * rows, half), jnp.bfloat16),
-            vmem((2 * steps * rows, 2 * groups * rows), jnp.float32),
+            vmem((2 * steps * rows, 128), jnp.float32),
             vmem((steps, rows, 128), jnp.float32),
-            vmem((plane, rows, 128), jnp.float32),
-            vmem((plane, rows, 128), jnp.float32),
-            vmem((steps, 8, 128), jnp.float32),
-            vmem((steps, 8, 128), jnp.float32),
-            dma((2,)),
+            vmem((steps * dims, rows // dims, 128), jnp.float32),
+            vmem((steps * plane, rows // dims, 128), jnp.float32),
+            dma((6,)),
             dma((2, chunks)),
             dma((3, chunks)),
             dma((steps, chunks)),
@@ -391,13 +412,11 @@
             dma((2 * groups, chunks)),
             dma((steps - 1,)),
             dma((steps,)),
-            dma((plane - 1,)),
-            dma((plane,)),
-            dma((steps - 1,)),
-            dma((steps,)),
+            dma((steps * plane - 1,)),
+            dma((steps * plane,)),
         ],
         compiler_params=pltpu.CompilerParams(
-            collective_id=0, has_side_effects=True, vmem_limit_bytes=32 * 1024 * 1024),
+            collective_id=0, has_side_effects=True, vmem_limit_bytes=60 * 1024 * 1024),
     )(
         query_grads, train_grads, example_ids.reshape(1, -1), query_ids.reshape(1, -1),
         query_norms.reshape(1, -1), train_norms.reshape(1, -1),

time: 71.2 us -> 62.7 us (0.88)
  local copies, waits for them, and re-layouts: 7.1 us -> 1.26 us
  Pallas kernels: 63.8 us -> 61.2 us
    unnamed x13 -> x1, local copies, waits for them, and re-layouts: 7.1 us -> 1.26 us
    pallas_call x1, Pallas kernels: 63.8 us -> 61.2 us  [all_pairs(): pl.pallas_call(functools.partial(kernel, sizes, width, wide), out_shape=j...]
where the time goes in v2:
time: 62.7 us; the launch traced here: 62.5 us
  Pallas kernels  61.2 us (98%)
  local copies, waits for them, and re-layouts  1.26 us (2%)
    pallas_call x1, Pallas kernels, all_pairs(): pl.pallas_call(functools.partial(kernel, sizes, width, wide), out_shape=j...  61.2 us
    unnamed x1, local copies, waits for them, and re-layouts  1.26 us

profile of v2, /device:TPU:0, one launch (start us, length us, event | category | flops | bytes accessed | tf_op | source)
XLA Modules:
  0.0 62.5 jit_solution(10598475837431523852)
XLA Ops:
  0.0 61.2 %shard_map.64 = f32[4,64]{1,0:T(4,128)} custom-call(f32[16,65536]{1,0:T(8,128)} %q_ref.1, bf16[16,65536]{1,0:T(8,128)(2,1)} %t_ref.1, s32[1,16]{1,0:T(1,128)} %bitcast.6, s32[1,4]{1,0:T(1,128)} %bitcast.7, f32[1,4096]{1,0:T(1,128)} %bitcast.4, f32[1,4096]{1,0:T(1,128)} %bitcast.5), custom_call_target="tpu_custom_call" | custom-call | tf_op jit(solution)/shard_map/pallas_call | solution.py:390
  61.3 1.3 %copy.8 = f32[4,64]{1,0:T(4,128)} copy(f32[4,64]{1,0:T(4,128)} %shard_map.64) | data formatting | bytes 2048

commit v3 on v2

--- a/solution.py
+++ b/solution.py
@@ -129,7 +129,36 @@
     peers.append((other_y, partner, d))
     for peer in peers:
         pl.semaphore_signal(barrier, inc=1, device_id=peer, device_id_type=MESH)
+    load_q.wait()
+
+    def largest(c, most):
+        return jnp.maximum(most, jnp.max(jnp.abs(qf[:, cols(c)]), axis=1, keepdims=True))
+
+    top = jnp.maximum(lax.fori_loop(0, chunks, largest, jnp.zeros((rows, 1), jnp.float32)), 1e-30)
+    scales[z] = jnp.broadcast_to(top * (1.0 / (FULL * FULL)), (rows, 128))
+    inverse = 1.0 / top
+
+    def encode(c):
+        x = qf[:, cols(c)]
+        size = (jnp.sqrt(jnp.abs(x) * inverse) * FULL + 0.5).astype(jnp.int32)
+        code[z, :, cols(c)] = jnp.where(x < 0, -size, size).astype(jnp.int16)
+
+    def send_wide(c):
+        @pl.when(is_inner)
+        def _():
+            send_code(z, c, far_inner, own_send.at[1, c]).start()
+
+        send_code(z, c, partner, own_send.at[0, c]).start()
+
+    def encode_wide(c, carry):
+        encode(c)
+        send_wide(c)
+        return carry
+
+    encode(0)
     pl.semaphore_wait(barrier, len(peers))
+    send_wide(0)
+    lax.fori_loop(1, wide, encode_wide, 0)
 
     @pl.when(is_inner)
     def _():
@@ -140,31 +169,6 @@
     def _():
         for args in across[:wide]:
             send_train(*args).start()
-
-    load_q.wait()
-
-    def largest(c, most):
-        return jnp.maximum(most, jnp.max(jnp.abs(qf[:, cols(c)]), axis=1, keepdims=True))
-
-    top = jnp.maximum(lax.fori_loop(0, chunks, largest, jnp.zeros((rows, 1), jnp.float32)), 1e-30)
-    scales[z] = jnp.broadcast_to(top * (1.0 / (FULL * FULL)), (rows, 128))
-    inverse = 1.0 / top
-
-    def encode(c):
-        x = qf[:, cols(c)]
-        size = (jnp.sqrt(jnp.abs(x) * inverse) * FULL + 0.5).astype(jnp.int32)
-        code[z, :, cols(c)] = jnp.where(x < 0, -size, size).astype(jnp.int16)
-
-    def encode_wide(c, carry):
-        encode(c)
-        send_code(z, c, partner, own_send.at[0, c]).start()
-
-        @pl.when(is_inner)
-        def _():
-            send_code(z, c, far_inner, own_send.at[1, c]).start()
-        return carry
-
-    lax.fori_loop(0, wide, encode_wide, 0)
 
     def send_scale(step):
         return remote(
@@ -231,6 +235,14 @@
         if at_y + at_z + at_d
     ]
 
+    offsets_z = [
+        at_z
+        for at_z in range(steps)
+        for at_y in range(groups)
+        for at_d in range(dims)
+        if at_y + at_z + at_d
+    ]
+
     def slot(peer):
         return (peer[0] * steps + peer[1]) * dims + peer[2]
 
@@ -239,25 +251,23 @@
     def send_tile(at):
         peer = peers_all[at]
         return remote(tiles.at[peer[1] * dims + peer[2]], tiles_in.at[place],
-                      tile_send.at[at], tile_recv.at[place], peer)
-
-    def got_tile(at):
-        peer = peers_all[at]
-        remote(tiles.at[peer[1] * dims + peer[2]], tiles_in.at[slot(peer)],
-               tile_send.at[at], tile_recv.at[slot(peer)], peer).wait_recv()
+                      tile_send.at[0], tile_recv.at[0], peer)
 
     def give_tiles():
         for step in range(1, steps):
             source = lax.rem(z + step, steps)
             remote(scales.at[source], scales.at[source], scale_send.at[0], scale_recv.at[source],
                    (y, source, d)).wait_recv()
-        for b in range(steps):
-            pieces = acc[pl.ds(b * rows, rows), :] + acc[pl.ds((steps + b) * rows, rows), :]
-            product = pieces * scales[b] + train_row
+        for at_z in (2, 1, 3, 0):
+            to_z = around[1][at_z]
+            upper = acc[pl.ds(pl.multiple_of(to_z * rows, rows), rows), :]
+            lower = acc[pl.ds(pl.multiple_of((steps + to_z) * rows, rows), rows), :]
+            product = (upper + lower) * scales[to_z] + train_row
             for to in range(dims):
-                tiles[b * dims + to] = product[to * mine:(to + 1) * mine]
-        for at in range(len(peers_all)):
-            send_tile(at).start()
+                tiles[to_z * dims + to] = product[to * mine:(to + 1) * mine]
+            for at, peer_z in enumerate(offsets_z):
+                if peer_z == at_z:
+                    send_tile(at).start()
         tiles_in[place] = tiles[z * dims + d]
 
     @pl.when(jnp.logical_not(is_inner))
@@ -275,6 +285,14 @@
 
         lax.fori_loop(0, wide, visit, 0)
         give_tiles()
+
+        def sent(c, carry):
+            send_code(z, c, partner, own_send.at[0, c]).wait_send()
+            return carry
+
+        lax.fori_loop(0, chunks, sent, 0)
+        for args in across[:wide] + straight[wide:] + diagonal[wide:]:
+            send_train(*args).wait_send()
 
     @pl.when(is_inner)
     def _():
@@ -320,8 +338,28 @@
         lax.fori_loop(wide, chunks, close, 0)
         give_tiles()
 
-    for at in range(len(peers_all)):
-        got_tile(at)
+        def sent(c, carry):
+            send_code(z, c, far_inner, own_send.at[1, c]).wait_send()
+            send_code(end, c, far_inner, fwd_send.at[0, c]).wait_send()
+            return carry
+
+        lax.fori_loop(0, chunks, sent, 0)
+
+        def sent_wide(c, carry):
+            send_code(z, c, end, own_send.at[0, c]).wait_send()
+            send_code(far_inner, c, end, fwd_send.at[1, c]).wait_send()
+            send_code(far_end, c, end, fwd_send.at[2, c]).wait_send()
+            return carry
+
+        lax.fori_loop(0, wide, sent_wide, 0)
+        for args in across:
+            send_train(*args).wait_send()
+
+    for step in range(1, steps):
+        send_scale(step).wait_send()
+    others = tiles_in.at[pl.ds(0, len(peers_all))]
+    all_tiles = remote(others, others, tile_send.at[0], tile_recv.at[0], peers_all[0])
+    all_tiles.wait_recv()
     by_source = tiles_in[...].reshape(groups, steps, dims, mine, 128)
     summed = jnp.sum(jnp.sum(by_source, axis=2), axis=0)
 
@@ -341,39 +379,7 @@
         scores = scores + jnp.where(here, jnp.concatenate([value] * steps, axis=1), 0.0)
     out_ref[...] = scores
 
-    @pl.when(jnp.logical_not(is_inner))
-    def _():
-        def sent(c, carry):
-            send_code(z, c, partner, own_send.at[0, c]).wait_send()
-            return carry
-
-        lax.fori_loop(0, chunks, sent, 0)
-        for args in across[:wide] + straight[wide:] + diagonal[wide:]:
-            send_train(*args).wait_send()
-
-    @pl.when(is_inner)
-    def _():
-        def sent(c, carry):
-            send_code(z, c, far_inner, own_send.at[1, c]).wait_send()
-            send_code(end, c, far_inner, fwd_send.at[0, c]).wait_send()
-            return carry
-
-        lax.fori_loop(0, chunks, sent, 0)
-
-        def sent_wide(c, carry):
-            send_code(z, c, end, own_send.at[0, c]).wait_send()
-            send_code(far_inner, c, end, fwd_send.at[1, c]).wait_send()
-            send_code(far_end, c, end, fwd_send.at[2, c]).wait_send()
-            return carry
-
-        lax.fori_loop(0, wide, sent_wide, 0)
-        for args in across:
-            send_train(*args).wait_send()
-
-    for step in range(1, steps):
-        send_scale(step).wait_send()
-    for at in range(len(peers_all)):
-        send_tile(at).wait_send()
+    all_tiles.wait_send()
 
 
 def all_pairs(sizes, query_grads, train_grads, example_ids, query_ids, query_norms, train_norms):
@@ -412,8 +418,8 @@
             dma((2 * groups, chunks)),
             dma((steps - 1,)),
             dma((steps,)),
-            dma((steps * plane - 1,)),
-            dma((steps * plane,)),
+            dma((1,)),
+            dma((1,)),
         ],
         compiler_params=pltpu.CompilerParams(
             collective_id=0, has_side_effects=True, vmem_limit_bytes=60 * 1024 * 1024),

time: 62.7 us -> 61.3 us (0.978)
  Pallas kernels: 61.2 us -> 59.9 us
    pallas_call x1, Pallas kernels: 61.2 us -> 59.9 us  [all_pairs(): pl.pallas_call(functools.partial(kernel, sizes, width, wide), out_shape=j...]
where the time goes in v3:
time: 61.3 us; the launch traced here: 61.2 us
  Pallas kernels  59.9 us (98%)
  local copies, waits for them, and re-layouts  1.26 us (2%)
    pallas_call x1, Pallas kernels, all_pairs(): pl.pallas_call(functools.partial(kernel, sizes, width, wide), out_shape=j...  59.9 us
    unnamed x1, local copies, waits for them, and re-layouts  1.26 us

profile of v3, /device:TPU:0, one launch (start us, length us, event | category | flops | bytes accessed | tf_op | source)
XLA Modules:
  0.0 61.2 jit_solution(9378992298767126740)
XLA Ops:
  0.0 59.9 %shard_map.64 = f32[4,64]{1,0:T(4,128)} custom-call(f32[16,65536]{1,0:T(8,128)} %q_ref.1, bf16[16,65536]{1,0:T(8,128)(2,1)} %t_ref.1, s32[1,16]{1,0:T(1,128)} %bitcast.6, s32[1,4]{1,0:T(1,128)} %bitcast.7, f32[1,4096]{1,0:T(1,128)} %bitcast.4, f32[1,4096]{1,0:T(1,128)} %bitcast.5), custom_call_target="tpu_custom_call" | custom-call | tf_op jit(solution)/shard_map/pallas_call | solution.py:396
  59.9 1.3 %copy.8 = f32[4,64]{1,0:T(4,128)} copy(f32[4,64]{1,0:T(4,128)} %shard_map.64) | data formatting | bytes 2048

commit v4 on v3

--- a/solution.py
+++ b/solution.py
@@ -221,6 +221,17 @@
             (((1,), (1,)), ((), ())), preferred_element_type=jnp.float32,
         )
 
+    def multiply_block(block, c, held):
+        coded = code[block, :, cols(c)].astype(jnp.int32).astype(jnp.float32)
+        value = coded * jnp.abs(coded)
+        upper = value.astype(jnp.bfloat16)
+        lower = (value - upper.astype(jnp.float32)).astype(jnp.bfloat16)
+        product = lax.dot_general(
+            jnp.concatenate([upper, lower], axis=0), tb[:held, cols(c)],
+            (((1,), (1,)), ((), ())), preferred_element_type=jnp.float32,
+        )
+        acc[pl.ds(pl.multiple_of(block * rows, rows), rows), :held] += product[:rows] + product[rows:]
+
     narrow = groups * rows
 
     around = [
@@ -253,11 +264,13 @@
         return remote(tiles.at[peer[1] * dims + peer[2]], tiles_in.at[place],
                       tile_send.at[0], tile_recv.at[0], peer)
 
-    def give_tiles():
+    def got_scales():
         for step in range(1, steps):
             source = lax.rem(z + step, steps)
             remote(scales.at[source], scales.at[source], scale_send.at[0], scale_recv.at[source],
                    (y, source, d)).wait_recv()
+
+    def give_tiles():
         for at_z in (2, 1, 3, 0):
             to_z = around[1][at_z]
             upper = acc[pl.ds(pl.multiple_of(to_z * rows, rows), rows), :]
@@ -284,6 +297,7 @@
             return carry
 
         lax.fori_loop(0, wide, visit, 0)
+        got_scales()
         give_tiles()
 
         def sent(c, carry):
@@ -335,7 +349,17 @@
             multiply(c, 2 * narrow)
             return carry
 
-        lax.fori_loop(wide, chunks, close, 0)
+        lax.fori_loop(wide, chunks - 1, close, 0)
+        got_scales()
+        last = chunks - 1
+        got_code(far_inner, last)
+        got_train(other_y, last)
+        got_train(2 + y, last)
+        got_train(2 + other_y, last)
+        for block in (z, end, far_inner):
+            multiply_block(block, last, 2 * narrow)
+        got_code(far_end, last)
+        multiply_block(far_end, last, 2 * narrow)
         give_tiles()
 
         def sent(c, carry):

time: 61.3 us -> 61.2 us (level)
  no operation moved by 1% of the time
where the time goes in v4:
time: 61.2 us; the launch traced here: 61 us
  Pallas kernels  59.7 us (98%)
  local copies, waits for them, and re-layouts  1.26 us (2%)
    pallas_call x1, Pallas kernels, all_pairs(): pl.pallas_call(functools.partial(kernel, sizes, width, wide), out_shape=j...  59.7 us
    unnamed x1, local copies, waits for them, and re-layouts  1.26 us

profile of v4, /device:TPU:0, one launch (start us, length us, event | category | flops | bytes accessed | tf_op | source)
XLA Modules:
  0.0 61.0 jit_solution(17603148556741802112)
XLA Ops:
  0.0 59.7 %shard_map.64 = f32[4,64]{1,0:T(4,128)} custom-call(f32[16,65536]{1,0:T(8,128)} %q_ref.1, bf16[16,65536]{1,0:T(8,128)(2,1)} %t_ref.1, s32[1,16]{1,0:T(1,128)} %bitcast.6, s32[1,4]{1,0:T(1,128)} %bitcast.7, f32[1,4096]{1,0:T(1,128)} %bitcast.4, f32[1,4096]{1,0:T(1,128)} %bitcast.5), custom_call_target="tpu_custom_call" | custom-call | tf_op jit(solution)/shard_map/pallas_call | solution.py:420
  59.7 1.3 %copy.8 = f32[4,64]{1,0:T(4,128)} copy(f32[4,64]{1,0:T(4,128)} %shard_map.64) | data formatting | bytes 2048
